TPU v7x, 512 devices: a whole 4x8x8 slice. The times are simulated.
512 devices in a mesh: users: 64 (over z, x, core), ctx: 8 (over y).
Axes of the slice: x: 4, y: 8, z: 8, core: 2. Of those that a mesh axis runs over, the one named last changes fastest.
Arguments:
- events: bfloat16 [32768, 1024], P(('users', 'ctx')), may hold values from -6 to 6
- owner_id: int32 [32768, 1], P(('users', 'ctx')), may hold values from 0 to 63; in each aligned block of 64 rows (0 to 63, 64 to 127, ...) at most 2 rows name the same one
- event_bucket: int32 [32768], P(('users', 'ctx')), may hold values from 0 to 31
- cross_weight: bfloat16 [1024, 1024], P('users'), may hold values from -0.1875 to 0.1875
- cross_bias: float32 [1024], replicated, may hold values from -3 to 3
- project_weight: bfloat16 [1024, 4096], P('users'), may hold values from -0.1875 to 0.1875
- cache_keys: bfloat16 [64, 8192, 1024], P('users', 'ctx'), may hold values from -6 to 6
- cache_values: bfloat16 [64, 8192, 1024], P('users', 'ctx'), may hold values from -60 to 60
- cache_length: int32 [64], P('users'), may hold values from 1024 to 8192
- cache_bucket: int32 [64, 8192], P('users', 'ctx'), may hold values from 0 to 31
- time_bias: float32 [32, 8], replicated, may hold values from -3 to 3
- norm_gain: float32 [1024], replicated, may hold values from 0.1 to 1.9
Outputs:
- gated: bfloat16 [32768, 1024], P(('users', 'ctx'))
Inputs may be any that keep to these rules, and one draw needn't show every extreme that they name: `owner_id`: no user is named by more than 2 of the 64 rows of one ingestion shard, and some user reaches that.
All inputs are finite; a program needn't handle non-finite values.
Results may differ from a plain program's by a relative error of at most 0.035.
Values may be sent and summed in bfloat16 or wider, within the bound.
A program may use at most 64 MiB of HBM per device.

v0:
```python
import jax
import jax.numpy as jnp
from jax import lax
from jax.sharding import PartitionSpec as P

H = 8
norm_epsilon = 1e-05


def from_everyone(value, axis):
    copies = jnp.broadcast_to(value, (lax.axis_size(axis), *value.shape))
    return lax.all_to_all(copies, axis, split_axis=0, concat_axis=0, tiled=True)


def in_order(parts, dim):
    parts = jnp.moveaxis(parts, 0, dim)
    dims = parts.shape
    return parts.reshape(*dims[:dim], dims[dim] * dims[dim + 1], *dims[dim + 2 :])


def gather_directly(value, axis, dim):
    parts = from_everyone(value, axis)
    return in_order(parts, dim)


def split_up(value, dim, peers):
    before, after = (value.shape[:dim], value.shape[dim + 1 :])
    return jnp.moveaxis(value.reshape(*before, peers, -1, *after), dim, 0)


def summed_on_arrival(value, axis, dim):
    parts = split_up(value, dim, lax.axis_size(axis))
    arrived = lax.all_to_all(parts, axis, split_axis=0, concat_axis=0, tiled=True)
    return arrived.astype(jnp.float32).sum(axis=0)


def bias_table(buckets, time_bias):
    levels = jnp.arange(time_bias.shape[0], dtype=jnp.int32)
    picked = (buckets[:, None] == levels[None, :]).astype(jnp.float32)
    return jnp.dot(picked, time_bias, precision=lax.Precision.HIGHEST)


def weighted_sum(keys_part, values_part, queries, key_bias, allowed, scale_factor):
    scores = jnp.einsum("khd,qhd->hkq", keys_part, queries, preferred_element_type=jnp.float32)
    scores = scores * scale_factor + key_bias.T[:, :, None]
    weights = jnp.where(allowed, jax.nn.silu(scores), 0.0).astype(jnp.bfloat16)
    return jnp.einsum("hkq,khd->qhd", weights, values_part, preferred_element_type=jnp.float32)


def shards(
    events,
    owner_id,
    event_bucket,
    cross_weight,
    cross_bias,
    project_weight,
    cache_keys,
    cache_values,
    cache_length,
    cache_bucket,
    time_bias,
    norm_gain,
):
    row_count, feature_width = events.shape
    head_count = H
    head_width = feature_width // head_count
    owner_count = lax.axis_size("users")
    context_count = lax.axis_size("ctx")
    context_index = lax.axis_index("ctx")
    capacity = max(2, (3 * row_count + 2 * owner_count - 1) // (2 * owner_count))
    slot_count = owner_count * capacity
    cache_rows = cache_keys.shape[1]
    scale_factor = head_width ** (-0.5)
    source = events.astype(jnp.float32)
    cross_full = gather_directly(cross_weight, "users", 0)
    crossing = jnp.dot(events, cross_full, preferred_element_type=jnp.float32)
    crossed = (source * (crossing + cross_bias) + source).astype(jnp.bfloat16)
    owners = owner_id[:, 0]
    positions = jnp.arange(row_count, dtype=jnp.int32)
    earlier = (owners[None, :] == owners[:, None]) & (positions[None, :] < positions[:, None])
    ranking = jnp.sum(earlier.astype(jnp.int32), axis=1)
    slot_of_row = owners * capacity + ranking
    placing = jnp.arange(slot_count, dtype=jnp.int32)[:, None] == slot_of_row[None, :]
    placing_matrix = placing.astype(jnp.bfloat16)
    outgoing = jnp.dot(placing_matrix, crossed, preferred_element_type=jnp.float32).astype(
        jnp.bfloat16
    )
    labels = jnp.sum(jnp.where(placing, event_bucket[None, :] + 1, 0), axis=1).astype(jnp.bfloat16)
    arrived, arrived_labels = (
        lax.all_to_all(
            outgoing.reshape(owner_count, capacity, feature_width),
            "users",
            split_axis=0,
            concat_axis=0,
            tiled=True,
        ),
        lax.all_to_all(
            labels.reshape(owner_count, capacity), "users", split_axis=0, concat_axis=0, tiled=True
        ),
    )
    arrived = arrived.reshape(slot_count, feature_width)
    label_values = arrived_labels.reshape(slot_count).astype(jnp.int32)
    project_full = lax.all_gather(project_weight, "users", axis=0, tiled=True)
    projected = jnp.dot(arrived, project_full, preferred_element_type=jnp.float32)
    activated = jax.nn.silu(projected)
    gate_units = activated[:, :feature_width].astype(jnp.bfloat16)
    new_values = (
        activated[:, feature_width : 2 * feature_width]
        .astype(jnp.bfloat16)
        .reshape(slot_count, head_count, head_width)
    )
    new_queries = activated[:, 2 * feature_width : 3 * feature_width].astype(jnp.bfloat16)
    new_keys = (
        activated[:, 3 * feature_width :]
        .astype(jnp.bfloat16)
        .reshape(slot_count, head_count, head_width)
    )
    slot_index = jnp.arange(slot_count, dtype=jnp.int32)
    key_order = (
        slot_index // capacity * context_count + context_index
    ) * capacity + slot_index % capacity
    key_valid = label_values > 0
    new_bias = bias_table(jnp.maximum(label_values - 1, 0), time_bias)
    cache_key_heads = cache_keys[0].reshape(cache_rows, head_count, head_width)
    cache_value_heads = cache_values[0].reshape(cache_rows, head_count, head_width)
    cache_bias = bias_table(cache_bucket[0], time_bias)
    live_length = cache_length[0] - context_index * cache_rows
    cache_live = jnp.arange(cache_rows, dtype=jnp.int32) < live_length
    block_keys = min(256, cache_rows)
    block_total = cache_rows // block_keys

    def attend_block(query_rows, query_start):
        block_rows = query_rows.shape[0]
        queries = query_rows.reshape(block_rows, head_count, head_width)
        query_index = query_start + jnp.arange(block_rows, dtype=jnp.int32)
        query_context = query_index // slot_count
        query_slot = query_index % slot_count
        query_order = (
            query_slot // capacity * context_count + query_context
        ) * capacity + query_slot % capacity
        allowed = key_valid[None, :, None] & (
            key_order[None, :, None] <= query_order[None, None, :]
        )
        summed = weighted_sum(new_keys, new_values, queries, new_bias, allowed, scale_factor)

        def add_block(block_number, carried):
            offset = block_number * block_keys
            keys_part = lax.dynamic_slice_in_dim(cache_key_heads, offset, block_keys, 0)
            values_part = lax.dynamic_slice_in_dim(cache_value_heads, offset, block_keys, 0)
            bias_part = lax.dynamic_slice_in_dim(cache_bias, offset, block_keys, 0)
            live_part = lax.dynamic_slice_in_dim(cache_live, offset, block_keys, 0)
            return carried + weighted_sum(
                keys_part, values_part, queries, bias_part, live_part[None, :, None], scale_factor
            )

        summed = lax.fori_loop(0, block_total, add_block, summed)
        return summed.reshape(block_rows, feature_width)

    query_piece = lax.all_gather(new_queries, "ctx", axis=0, tiled=True)
    piece_rows = query_piece.shape[0]
    block_count = piece_rows // 512
    stacked = query_piece.reshape(block_count, 512, feature_width)
    block_starts = 512 * jnp.arange(block_count, dtype=jnp.int32)

    def one_block(bundle):
        return attend_block(bundle[0], bundle[1])

    outputs = lax.map(one_block, (stacked, block_starts))
    partials = outputs.reshape(piece_rows, feature_width)
    attended = summed_on_arrival(partials.astype(jnp.bfloat16), "ctx", 0)
    center = jnp.mean(attended, axis=1, keepdims=True)
    spread = jnp.mean(jnp.square(attended - center), axis=1, keepdims=True)
    normed = (attended - center) * lax.rsqrt(spread + norm_epsilon)
    gated = (normed * norm_gain * gate_units.astype(jnp.float32)).astype(jnp.bfloat16)
    returned = lax.all_to_all(
        gated.reshape(owner_count, capacity, feature_width),
        "users",
        split_axis=0,
        concat_axis=0,
        tiled=True,
    )
    result = lax.dot_general(
        placing_matrix,
        returned.reshape(slot_count, feature_width),
        (((0,), (0,)), ((), ())),
        preferred_element_type=jnp.float32,
    )
    return result.astype(jnp.bfloat16)


def solution(mesh):
    return jax.shard_map(
        shards,
        mesh=mesh,
        in_specs=(
            P(("users", "ctx"), None),
            P(("users", "ctx"), None),
            P(("users", "ctx")),
            P("users", None),
            P(),
            P("users", None),
            P("users", "ctx", None),
            P("users", "ctx", None),
            P("users"),
            P("users", "ctx"),
            P(),
            P(),
        ),
        out_specs=P(("users", "ctx"), None),
        check_vma=False,
    )
```

profile of v0, /device:TPU:1, one launch (start us, length us, event | category | flops | bytes accessed | tf_op | source)
XLA Modules:
  0.0 300.3 jit_solution(16034690586346479970)
XLA Ops:
  9.6 15.0 %all-to-all-start.1 = ((bf16[64,16,1024]{2,1,0:T(8,128)(2,1)}), bf16[64,16,1024]{2,1,0:T(8,128)(2,1)S(1)}, u32[]{:S(2)}, u32[]{:S(2)}) async-start(bf16[64,16,1024]{2,1,0:T(8,128)(2,1)} %broadcast_in_dim.96), calls=%async_computation.1 | async-start | bytes 4194304 | tf_op jit(solution)/shard_map/all_to_all | solution.py:12
  24.9 54.3 %all-to-all-done.1 = bf16[64,16,1024]{2,1,0:T(8,128)(2,1)S(1)} async-done(((bf16[64,16,1024]{2,1,0:T(8,128)(2,1)}), bf16[64,16,1024]{2,1,0:T(8,128)(2,1)S(1)}, u32[]{:S(2)}, u32[]{:S(2)}) %all-to-all-start.1) | async-done | bytes 2097184 | tf_op jit(solution)/shard_map/all_to_all | solution.py:12
  80.0 21.7 %all_to_all.26 = bf16[64,2,1024]{2,1,0:T(2,128)(2,1)S(1)} all-to-all(bf16[64,2,1024]{2,1,0:T(2,128)(2,1)S(1)} %reshape.197), channel_id=1, replica_groups=mesh['users'=64,'ctx'=8] {'users'}, dimensions={0} | all-to-all | bytes 524288 | tf_op jit(solution)/shard_map/all_to_all | solution.py:90
  101.8 14.6 %all-gather.3.cloned.1.call-done = bf16[1024,4096]{1,0:T(8,128)(2,1)} async-done(((bf16[16,4096]{1,0:T(8,128)(2,1)}), bf16[1024,4096]{1,0:T(8,128)(2,1)}) %all-gather.3.cloned.1.call-update) | async-done | bytes 8388624 | tf_op jit(solution)/shard_map/all_gather | solution.py:103
  116.5 4.7 %multiply_convert_fusion = bf16[128,4096]{1,0:T(8,128)(2,1)S(1)} fusion(bf16[128,1024]{1,0:T(8,128)(2,1)S(1)} %reshape.198, bf16[1024,4096]{1,0:T(8,128)(2,1)} %all-gather.3.cloned.1.call-done), kind=kOutput, calls=%fused_computation.63 | convolution fusion | flops 1076363264 | bytes 9699328 | tf_op jit(solution)/shard_map/dot_general | solution.py:104
  124.0 7.0 %all-to-all-start = ((bf16[64,1,2]{2,1,0:T(2,128)(2,1)}), bf16[64,1,2]{2,1,0:T(2,128)(2,1)S(1)}, u32[]{:S(2)}, u32[]{:S(2)}) async-start(bf16[64,1,2]{2,1,0:T(2,128)(2,1)} %convert_element_type.88), calls=%async_computation | async-start | bytes 65536 | tf_op jit(solution)/shard_map/all_to_all | solution.py:97
  131.6 2.9 copy.43
  137.3 3.9 %copy.42 = bf16[1,1024,1024]{1,2,0:T(8,128)(2,1)} copy(bf16[1,1024,1024]{2,1,0:T(8,128)(2,1)} %param.23) | data formatting | bytes 4194304 | tf_op args[7]
  142.2 18.1 %all-gather.5.cloned.1.call-done = bf16[1024,1024]{1,0:T(8,128)(2,1)} async-done(((bf16[128,1024]{1,0:T(8,128)(2,1)}), bf16[1024,1024]{1,0:T(8,128)(2,1)}) %all-gather.5.cloned.1.call-update) | async-done | bytes 2097168 | tf_op jit(solution)/shard_map/all_gather | solution.py:159
  160.3 50.7 %while.38 = (s32[]{:T(128)}, bf16[2,512,1024]{2,1,0:T(8,128)(2,1)}, pred[128]{0:T(512)(128)(4,1)S(1)}, s32[2]{0:T(128)S(1)}, bf16[2,512,1024]{2,1,0:T(8,128)(2,1...) while((s32[]{:T(128)}, bf16[2,512,1024]{2,1,0:T(8,128)(2,1)}, ...), condition=%wide.region_5.6_spmd.clone, body=%wide.region_2.5_spmd.clone.sunk | while | flops 818569728 | bytes 27956100 | solution.py:168
  163.6 2.5 convolution_bitcast_fusion.2
  169.3 14.6 %while.39 = (s32[]{:T(128)}, f32[512,8,128]{0,2,1:T(8,128)S(1)}, bf16[1024,8,128]{0,2,1:T(8,128)(2,1)}, pred[1024]{0:T(1024)(128)(4,1)S(1)}, bf16[1024,8,128]{2,...) while((s32[]{:T(128)}, f32[512,8,128]{0,2,1:T(8,128)S(1)}, ...), condition=%wide.region_4.4_spmd, body=%wide.region_3.3_spmd.sunk | while | flops 545783808 | bytes 6317987 | solution.py:156
  169.4 3.5 %bitcast_add_fusion.2 = f32[512,8,128]{0,2,1:T(8,128)S(1)} fusion(f32[512,8,128]{0,2,1:T(8,128)S(1)} %get-tuple-element.659, bf16[512,8,128]{2,0,1:T(8,128)(2,1)} %get-tuple-element.674, f32[8,256]{1,0:T(8,128)S(1)} %dynamic-slice_bitcast_fusion.2, pred[256]{0:T(512)(128)(4,1)S(1)} %dynamic_slice.64, bf16[1024,8,128]{2,0,1:T(8,128)(2,1)} %get-tuple-element.673, ...), kind=kOutput, calls=%fused_computation.3.clone.1 | convolution fusion | flops 545783808 | bytes 6300928 | tf_op jit(solution)/shard_map/while/body/eval_jaxpr/while/body/eval_jaxpr/hkq,khd->qhd/dot_general | solution.py:47
  173.1 3.5 %bitcast_add_fusion.2 = f32[512,8,128]{0,2,1:T(8,128)S(1)} fusion(f32[512,8,128]{0,2,1:T(8,128)S(1)} %get-tuple-element.659, bf16[512,8,128]{2,0,1:T(8,128)(2,1)} %get-tuple-element.674, f32[8,256]{1,0:T(8,128)S(1)} %dynamic-slice_bitcast_fusion.2, pred[256]{0:T(512)(128)(4,1)S(1)} %dynamic_slice.64, bf16[1024,8,128]{2,0,1:T(8,128)(2,1)} %get-tuple-element.673, ...), kind=kOutput, calls=%fused_computation.3.clone.1 | convolution fusion | flops 545783808 | bytes 6300928 | tf_op jit(solution)/shard_map/while/body/eval_jaxpr/while/body/eval_jaxpr/hkq,khd->qhd/dot_general | solution.py:47
  176.7 3.5 %bitcast_add_fusion.2 = f32[512,8,128]{0,2,1:T(8,128)S(1)} fusion(f32[512,8,128]{0,2,1:T(8,128)S(1)} %get-tuple-element.659, bf16[512,8,128]{2,0,1:T(8,128)(2,1)} %get-tuple-element.674, f32[8,256]{1,0:T(8,128)S(1)} %dynamic-slice_bitcast_fusion.2, pred[256]{0:T(512)(128)(4,1)S(1)} %dynamic_slice.64, bf16[1024,8,128]{2,0,1:T(8,128)(2,1)} %get-tuple-element.673, ...), kind=kOutput, calls=%fused_computation.3.clone.1 | convolution fusion | flops 545783808 | bytes 6300928 | tf_op jit(solution)/shard_map/while/body/eval_jaxpr/while/body/eval_jaxpr/hkq,khd->qhd/dot_general | solution.py:47
  180.4 3.5 %bitcast_add_fusion.2 = f32[512,8,128]{0,2,1:T(8,128)S(1)} fusion(f32[512,8,128]{0,2,1:T(8,128)S(1)} %get-tuple-element.659, bf16[512,8,128]{2,0,1:T(8,128)(2,1)} %get-tuple-element.674, f32[8,256]{1,0:T(8,128)S(1)} %dynamic-slice_bitcast_fusion.2, pred[256]{0:T(512)(128)(4,1)S(1)} %dynamic_slice.64, bf16[1024,8,128]{2,0,1:T(8,128)(2,1)} %get-tuple-element.673, ...), kind=kOutput, calls=%fused_computation.3.clone.1 | convolution fusion | flops 545783808 | bytes 6300928 | tf_op jit(solution)/shard_map/while/body/eval_jaxpr/while/body/eval_jaxpr/hkq,khd->qhd/dot_general | solution.py:47
  188.9 2.5 convolution_bitcast_fusion.2
  194.7 14.6 %while.39 = (s32[]{:T(128)}, f32[512,8,128]{0,2,1:T(8,128)S(1)}, bf16[1024,8,128]{0,2,1:T(8,128)(2,1)}, pred[1024]{0:T(1024)(128)(4,1)S(1)}, bf16[1024,8,128]{2,...) while((s32[]{:T(128)}, f32[512,8,128]{0,2,1:T(8,128)S(1)}, ...), condition=%wide.region_4.4_spmd, body=%wide.region_3.3_spmd.sunk | while | flops 545783808 | bytes 6317987 | solution.py:156
  194.7 3.5 %bitcast_add_fusion.2 = f32[512,8,128]{0,2,1:T(8,128)S(1)} fusion(f32[512,8,128]{0,2,1:T(8,128)S(1)} %get-tuple-element.659, bf16[512,8,128]{2,0,1:T(8,128)(2,1)} %get-tuple-element.674, f32[8,256]{1,0:T(8,128)S(1)} %dynamic-slice_bitcast_fusion.2, pred[256]{0:T(512)(128)(4,1)S(1)} %dynamic_slice.64, bf16[1024,8,128]{2,0,1:T(8,128)(2,1)} %get-tuple-element.673, ...), kind=kOutput, calls=%fused_computation.3.clone.1 | convolution fusion | flops 545783808 | bytes 6300928 | tf_op jit(solution)/shard_map/while/body/eval_jaxpr/while/body/eval_jaxpr/hkq,khd->qhd/dot_general | solution.py:47
  198.4 3.5 %bitcast_add_fusion.2 = f32[512,8,128]{0,2,1:T(8,128)S(1)} fusion(f32[512,8,128]{0,2,1:T(8,128)S(1)} %get-tuple-element.659, bf16[512,8,128]{2,0,1:T(8,128)(2,1)} %get-tuple-element.674, f32[8,256]{1,0:T(8,128)S(1)} %dynamic-slice_bitcast_fusion.2, pred[256]{0:T(512)(128)(4,1)S(1)} %dynamic_slice.64, bf16[1024,8,128]{2,0,1:T(8,128)(2,1)} %get-tuple-element.673, ...), kind=kOutput, calls=%fused_computation.3.clone.1 | convolution fusion | flops 545783808 | bytes 6300928 | tf_op jit(solution)/shard_map/while/body/eval_jaxpr/while/body/eval_jaxpr/hkq,khd->qhd/dot_general | solution.py:47
  202.1 3.5 %bitcast_add_fusion.2 = f32[512,8,128]{0,2,1:T(8,128)S(1)} fusion(f32[512,8,128]{0,2,1:T(8,128)S(1)} %get-tuple-element.659, bf16[512,8,128]{2,0,1:T(8,128)(2,1)} %get-tuple-element.674, f32[8,256]{1,0:T(8,128)S(1)} %dynamic-slice_bitcast_fusion.2, pred[256]{0:T(512)(128)(4,1)S(1)} %dynamic_slice.64, bf16[1024,8,128]{2,0,1:T(8,128)(2,1)} %get-tuple-element.673, ...), kind=kOutput, calls=%fused_computation.3.clone.1 | convolution fusion | flops 545783808 | bytes 6300928 | tf_op jit(solution)/shard_map/while/body/eval_jaxpr/while/body/eval_jaxpr/hkq,khd->qhd/dot_general | solution.py:47
  205.7 3.5 %bitcast_add_fusion.2 = f32[512,8,128]{0,2,1:T(8,128)S(1)} fusion(f32[512,8,128]{0,2,1:T(8,128)S(1)} %get-tuple-element.659, bf16[512,8,128]{2,0,1:T(8,128)(2,1)} %get-tuple-element.674, f32[8,256]{1,0:T(8,128)S(1)} %dynamic-slice_bitcast_fusion.2, pred[256]{0:T(512)(128)(4,1)S(1)} %dynamic_slice.64, bf16[1024,8,128]{2,0,1:T(8,128)(2,1)} %get-tuple-element.673, ...), kind=kOutput, calls=%fused_computation.3.clone.1 | convolution fusion | flops 545783808 | bytes 6300928 | tf_op jit(solution)/shard_map/while/body/eval_jaxpr/while/body/eval_jaxpr/hkq,khd->qhd/dot_general | solution.py:47
  211.0 49.5 %all_to_all.27 = bf16[8,128,1024]{2,1,0:T(8,128)(2,1)S(1)} all-to-all(bf16[8,128,1024]{2,1,0:T(8,128)(2,1)} %bitcast.87), channel_id=1, replica_groups=mesh['users'=64,'ctx'=8] {'ctx'}, dimensions={0} | all-to-all | bytes 4194304 | tf_op jit(solution)/shard_map/all_to_all | solution.py:33
  262.5 30.0 %all_to_all.28 = bf16[64,2,1024]{2,1,0:T(2,128)(2,1)S(1)} all-to-all(bf16[64,2,1024]{2,1,0:T(2,128)(2,1)S(1)} %reshape.202), channel_id=1, replica_groups=mesh['users'=64,'ctx'=8] {'users'}, dimensions={0} | all-to-all | bytes 524288 | tf_op jit(solution)/shard_map/all_to_all | solution.py:175
  (100 shorter events, 30.7 us)
Async XLA Ops:
  6.5 127.9 %copy-start = (f32[32,8]{0,1:T(8,128)S(1)}, f32[32,8]{0,1:T(8,128)}, u32[]{:S(2)}) copy-start(f32[32,8]{0,1:T(8,128)} %param.26) | copy-start | bytes 3076
  6.5 109.9 %all-gather.3.cloned.1.call-start = ((), (), s32[]{:S(2)}) async-start(), calls=%async_computation.5 | async-start | bytes 8519680 | tf_op jit(solution)/shard_map/all_gather | solution.py:103
  9.6 15.0 %copy-start.10 = (s32[64,1]{0,1:T(1,128)S(1)}, s32[64,1]{0,1:T(1,128)}, u32[]{:S(2)}) copy-start(s32[64,1]{0,1:T(1,128)} %param.17) | copy-start | bytes 772
  9.6 69.6 %copy-start.4 = (bf16[64,1024]{1,0:T(8,128)(2,1)S(1)}, bf16[64,1024]{1,0:T(8,128)(2,1)}, u32[]{:S(2)}) copy-start(bf16[64,1024]{1,0:T(8,128)(2,1)} %param.16) | copy-start | bytes 393220
  9.6 69.6 %copy-start.5 = (f32[1024]{0:T(1024)S(1)}, f32[1024]{0:T(1024)}, u32[]{:S(2)}) copy-start(f32[1024]{0:T(1024)} %param.20) | copy-start | bytes 12292
  9.6 69.6 %all-to-all-start.1 = ((bf16[64,16,1024]{2,1,0:T(8,128)(2,1)}), bf16[64,16,1024]{2,1,0:T(8,128)(2,1)S(1)}, u32[]{:S(2)}, u32[]{:S(2)}) async-start(bf16[64,16,1024]{2,1,0:T(8,128)(2,1)} %broadcast_in_dim.96), calls=%async_computation.1 | async-start | bytes 4194304 | tf_op jit(solution)/shard_map/all_to_all | solution.py:12
  24.6 135.7 %all-gather.5.cloned.1.call-start = ((), (), s32[]{:S(2)}) async-start(), calls=%async_computation.6 | async-start | bytes 2359296 | tf_op jit(solution)/shard_map/all_gather | solution.py:159
  24.9 98.2 %copy-start.7 = (s32[64]{0:T(128)}, s32[64]{0:T(128)S(1)}, u32[]{:S(2)}) copy-start(s32[64]{0:T(128)S(1)} %multiply_add_fusion) | copy-start | bytes 772
  101.8 21.2 %copy-start.11 = (s32[64]{0:T(128)S(1)}, s32[64]{0:T(128)}, u32[]{:S(2)}) copy-start(s32[64]{0:T(128)} %param.18) | copy-start | bytes 772
  121.2 1.0 copy-start.1
  124.0 17.3 %all-to-all-start = ((bf16[64,1,2]{2,1,0:T(2,128)(2,1)}), bf16[64,1,2]{2,1,0:T(2,128)(2,1)S(1)}, u32[]{:S(2)}, u32[]{:S(2)}) async-start(bf16[64,1,2]{2,1,0:T(2,128)(2,1)} %convert_element_type.88), calls=%async_computation | async-start | bytes 65536 | tf_op jit(solution)/shard_map/all_to_all | solution.py:97
  131.6 2.9 copy-start.9
  160.3 3.3 %copy-start.2 = (bf16[128,8,128]{2,0,1:T(8,128)(2,1)}, bf16[128,8,128]{2,0,1:T(8,128)(2,1)S(1)}, u32[]{:S(2)}) copy-start(bf16[128,8,128]{2,0,1:T(8,128)(2,1)S(1)} %get-tuple-element.723) | copy-start | bytes 786436 | tf_op jit(solution)/shard_map/while
  184.5 1.1 copy-start.3
  185.6 3.3 %copy-start.2 = (bf16[128,8,128]{2,0,1:T(8,128)(2,1)}, bf16[128,8,128]{2,0,1:T(8,128)(2,1)S(1)}, u32[]{:S(2)}) copy-start(bf16[128,8,128]{2,0,1:T(8,128)(2,1)S(1)} %get-tuple-element.723) | copy-start | bytes 786436 | tf_op jit(solution)/shard_map/while
  209.9 1.1 copy-start.3
  260.5 0.7 copy-start.6
  261.0 31.6 %copy-start.8 = (s32[64]{0:T(128)S(1)}, s32[64]{0:T(128)}, u32[]{:S(2)}) copy-start(s32[64]{0:T(128)} %copy-done.7) | copy-start | bytes 772
Sparse Core Ops, SparseCore 0:
  10.7 105.7 all-gather.2
  123.1 37.1 all-gather.4
where the time goes:
time: 301 us; the launch traced here: 300 us
  blocking collectives  101 us (34%)
  waiting for transfers between devices  87.8 us (29%)
  matrix products  40.1 us (13%)
  local copies, waits for them, and re-layouts  30.5 us (10%)
  starting transfers between devices  22 us (7%)
  between operations  14.3 us (5%)
  other arithmetic  4.04 us (1%)
    all_to_all x1, waiting for transfers between devices, from_everyone(): return lax.all_to_all(copies, axis, split_axis=0, concat_axis=0, tiled=True)  54.3 us
    all_to_all x1, blocking collectives, summed_on_arrival(): lax.all_to_all(parts, axis, split_axis=0, concat_axis=0, tiled=True)  49.5 us
    dot_general x10, matrix products, weighted_sum(): jnp.einsum('hkq,khd->qhd', weights, values_part, preferred_element_type=j...  33.2 us
    all_to_all x1, blocking collectives, shards(): lax.all_to_all(gated.reshape(owner_count, capacity, feature_width), 'user...  30 us
    all_to_all x1, blocking collectives, shards(): lax.all_to_all(outgoing.reshape(owner_count, capacity, feature_width), 'u...  21.7 us
    all_gather x1, waiting for transfers between devices, shards(): query_piece = lax.all_gather(new_queries, 'ctx', axis=0, tiled=True)  18.1 us
    all_to_all x1, starting transfers between devices, from_everyone(): return lax.all_to_all(copies, axis, split_axis=0, concat_axis=0, tiled=True)  15 us
    all_gather x1, waiting for transfers between devices, shards(): project_full = lax.all_gather(project_weight, 'users', axis=0, tiled=True)  14.6 us
  transfers between devices with their start and end apart: 4, of which 3 were waited for; matrix products, arithmetic and copies ran while one was open for 5% of the time, Pallas kernels for 0%

commit v1 on v0

--- a/solution.py
+++ b/solution.py
@@ -156,7 +156,10 @@
         summed = lax.fori_loop(0, block_total, add_block, summed)
         return summed.reshape(block_rows, feature_width)
 
-    query_piece = lax.all_gather(new_queries, "ctx", axis=0, tiled=True)
+    count = lax.axis_size("ctx")
+    blocks = jnp.stack([new_queries for _ in range(count)])
+    blocks = lax.all_to_all(blocks, "ctx", split_axis=0, concat_axis=0)
+    query_piece = jnp.concatenate(blocks, axis=0)
     piece_rows = query_piece.shape[0]
     block_count = piece_rows // 512
     stacked = query_piece.reshape(block_count, 512, feature_width)

time: 301 us -> 317 us (1.053)
  waiting for transfers between devices: 87.8 us -> 115 us
  blocking collectives: 101 us -> 75.7 us
  starting transfers between devices: 22 us -> 33.6 us
    all_to_all x0 -> x2, waiting for transfers between devices: none -> 51.6 us  [the longest x1 37.1 us: shards(): blocks = lax.all_to_all(blocks, 'ctx', split_axis=0, concat_axis=0)]
    all_to_all x1 -> x0, blocking collectives: 21.7 us -> none  [shards(): lax.all_to_all(outgoing.reshape(owner_count, capacity, feature_width), 'u...]
    all_gather x1 -> x0, waiting for transfers between devices: 18.1 us -> none  [shards(): query_piece = lax.all_gather(new_queries, 'ctx', axis=0, tiled=True)]
    all_to_all x0 -> x2, starting transfers between devices: none -> 13.8 us  [the longest x1 7.02 us: shards(): lax.all_to_all(outgoing.reshape(owner_count, capacity, feature_width), 'u...]
    all_to_all x1, blocking collectives: 30 us -> 22.9 us  [shards(): lax.all_to_all(gated.reshape(owner_count, capacity, feature_width), 'user...]
    all_gather x1, waiting for transfers between devices: 14.6 us -> 8.63 us  [shards(): project_full = lax.all_gather(project_weight, 'users', axis=0, tiled=True)]
    all_to_all x1, blocking collectives: 49.5 us -> 52.8 us  [summed_on_arrival(): lax.all_to_all(parts, axis, split_axis=0, concat_axis=0, tiled=True)]
  transfers between devices with their start and end apart: 4 -> 5, of which waited for: 3 -> 4; matrix products, arithmetic and copies ran while one was open for 5% -> 6% of each run, Pallas kernels for 0% -> 0%
where the time goes in v1:
time: 317 us; the launch traced here: 316 us
  waiting for transfers between devices  115 us (36%)
  blocking collectives  75.7 us (24%)
  matrix products  40.1 us (13%)
  starting transfers between devices  33.6 us (11%)
  local copies, waits for them, and re-layouts  32.2 us (10%)
  between operations  14.2 us (4%)
  other arithmetic  4.1 us (1%)
    all_to_all x1, waiting for transfers between devices, from_everyone(): return lax.all_to_all(copies, axis, split_axis=0, concat_axis=0, tiled=True)  54.4 us
    all_to_all x1, blocking collectives, summed_on_arrival(): lax.all_to_all(parts, axis, split_axis=0, concat_axis=0, tiled=True)  52.8 us
    all_to_all x1, waiting for transfers between devices, shards(): blocks = lax.all_to_all(blocks, 'ctx', split_axis=0, concat_axis=0)  37.1 us
    dot_general x10, matrix products, weighted_sum(): jnp.einsum('hkq,khd->qhd', weights, values_part, preferred_element_type=j...  33.2 us
    all_to_all x1, blocking collectives, shards(): lax.all_to_all(gated.reshape(owner_count, capacity, feature_width), 'user...  22.9 us
    all_to_all x1, starting transfers between devices, from_everyone(): return lax.all_to_all(copies, axis, split_axis=0, concat_axis=0, tiled=True)  15 us
    all_to_all x1, waiting for transfers between devices, shards(): lax.all_to_all(outgoing.reshape(owner_count, capacity, feature_width), 'u...  14.4 us
    unnamed x25, local copies, waits for them, and re-layouts  10.4 us
  transfers between devices with their start and end apart: 5, of which 4 were waited for; matrix products, arithmetic and copies ran while one was open for 6% of the time, Pallas kernels for 0%

profile of v1, /device:TPU:1, one launch (start us, length us, event | category | flops | bytes accessed | tf_op | source)
XLA Modules:
  0.0 315.7 jit_solution(11716987560286439453)
XLA Ops:
  9.6 15.0 %all-to-all-start.1 = ((bf16[64,16,1024]{2,1,0:T(8,128)(2,1)}), bf16[64,16,1024]{2,1,0:T(8,128)(2,1)S(1)}, u32[]{:S(2)}, u32[]{:S(2)}) async-start(bf16[64,16,1024]{2,1,0:T(8,128)(2,1)} %broadcast_in_dim.96), calls=%async_computation.1 | async-start | bytes 4194304 | tf_op jit(solution)/shard_map/all_to_all | solution.py:12
  24.8 54.4 %all-to-all-done.1 = bf16[64,16,1024]{2,1,0:T(8,128)(2,1)S(1)} async-done(((bf16[64,16,1024]{2,1,0:T(8,128)(2,1)}), bf16[64,16,1024]{2,1,0:T(8,128)(2,1)S(1)}, u32[]{:S(2)}, u32[]{:S(2)}) %all-to-all-start.1) | async-done | bytes 2097184 | tf_op jit(solution)/shard_map/all_to_all | solution.py:12
  80.7 7.0 %all-to-all-start.2 = ((bf16[64,2,1024]{2,1,0:T(2,128)(2,1)}), bf16[64,2,1024]{2,1,0:T(2,128)(2,1)S(1)}, u32[]{:S(2)}, u32[]{:S(2)}) async-start(bf16[64,2,1024]{2,1,0:T(2,128)(2,1)} %reshape.196), calls=%async_computation.2 | async-start | bytes 524288 | tf_op jit(solution)/shard_map/all_to_all | solution.py:90
  88.7 14.4 %all-to-all-done.2 = bf16[64,2,1024]{2,1,0:T(2,128)(2,1)S(1)} async-done(((bf16[64,2,1024]{2,1,0:T(2,128)(2,1)}), bf16[64,2,1024]{2,1,0:T(2,128)(2,1)S(1)}, u32[]{:S(2)}, u32[]{:S(2)}) %all-to-all-start.2) | async-done | bytes 262176 | tf_op jit(solution)/shard_map/all_to_all | solution.py:90
  103.1 4.9 %all-to-all-start = ((bf16[64,1,2]{2,1,0:T(2,128)(2,1)}), bf16[64,1,2]{2,1,0:T(2,128)(2,1)S(1)}, u32[]{:S(2)}, u32[]{:S(2)}) async-start(bf16[64,1,2]{2,1,0:T(2,128)(2,1)} %convert_element_type.88), calls=%async_computation | async-start | bytes 65536 | tf_op jit(solution)/shard_map/all_to_all | solution.py:97
  108.1 8.6 %all-gather.2.cloned.1.call-done = bf16[1024,4096]{1,0:T(8,128)(2,1)} async-done(((bf16[16,4096]{1,0:T(8,128)(2,1)}), bf16[1024,4096]{1,0:T(8,128)(2,1)}) %all-gather.2.cloned.1.call-update) | async-done | bytes 8388624 | tf_op jit(solution)/shard_map/all_gather | solution.py:103
  116.7 4.7 %multiply_convert_fusion = bf16[128,4096]{1,0:T(8,128)(2,1)S(1)} fusion(bf16[128,1024]{1,0:T(8,128)(2,1)S(1)} %reshape.197, bf16[1024,4096]{1,0:T(8,128)(2,1)} %all-gather.2.cloned.1.call-done), kind=kOutput, calls=%fused_computation.63 | convolution fusion | flops 1076363264 | bytes 9699328 | tf_op jit(solution)/shard_map/dot_general | solution.py:104
  124.2 6.7 %all-to-all-start.3 = ((bf16[8,128,1024]{2,1,0:T(8,128)(2,1)}), bf16[8,128,1024]{2,1,0:T(8,128)(2,1)}, u32[]{:S(2)}, u32[]{:S(2)}) async-start(bf16[8,128,1024]{2,1,0:T(8,128)(2,1)} %stack.2), calls=%async_computation.3 | async-start | bytes 4194304 | tf_op jit(solution)/shard_map/all_to_all | solution.py:161
  131.6 2.9 copy.52
  136.8 3.9 %copy.51 = bf16[1,1024,1024]{1,2,0:T(8,128)(2,1)} copy(bf16[1,1024,1024]{2,1,0:T(8,128)(2,1)} %param.23) | data formatting | bytes 4194304 | tf_op args[7]
  142.2 37.1 %all-to-all-done.3 = bf16[8,128,1024]{2,1,0:T(8,128)(2,1)} async-done(((bf16[8,128,1024]{2,1,0:T(8,128)(2,1)}), bf16[8,128,1024]{2,1,0:T(8,128)(2,1)}, u32[]{:S(2)}, u32[]{:S(2)}) %all-to-all-start.3) | async-done | bytes 2097184 | tf_op jit(solution)/shard_map/all_to_all | solution.py:161
  179.3 50.8 %while.38 = (s32[]{:T(128)}, bf16[2,512,1024]{2,1,0:T(8,128)(2,1)}, pred[128]{0:T(512)(128)(4,1)S(1)}, s32[2]{0:T(128)S(1)}, bf16[2,512,1024]{2,1,0:T(8,128)(2,1...) while((s32[]{:T(128)}, bf16[2,512,1024]{2,1,0:T(8,128)(2,1)}, ...), condition=%wide.region_5.6_spmd.clone, body=%wide.region_2.5_spmd.clone.sunk | while | flops 818569728 | bytes 27956100 | solution.py:171
  188.4 14.6 %while.39 = (s32[]{:T(128)}, f32[512,8,128]{0,2,1:T(8,128)S(1)}, bf16[1024,8,128]{0,2,1:T(8,128)(2,1)}, pred[1024]{0:T(1024)(128)(4,1)S(1)}, bf16[1024,8,128]{2,...) while((s32[]{:T(128)}, f32[512,8,128]{0,2,1:T(8,128)S(1)}, ...), condition=%wide.region_4.4_spmd, body=%wide.region_3.3_spmd.sunk | while | flops 545783808 | bytes 6317987 | solution.py:156
  188.5 3.5 %bitcast_add_fusion.2 = f32[512,8,128]{0,2,1:T(8,128)S(1)} fusion(f32[512,8,128]{0,2,1:T(8,128)S(1)} %get-tuple-element.679, bf16[512,8,128]{2,0,1:T(8,128)(2,1)} %get-tuple-element.694, f32[8,256]{1,0:T(8,128)S(1)} %dynamic-slice_bitcast_fusion.2, pred[256]{0:T(512)(128)(4,1)S(1)} %dynamic_slice.64, bf16[1024,8,128]{2,0,1:T(8,128)(2,1)} %get-tuple-element.693, ...), kind=kOutput, calls=%fused_computation.3.clone.1 | convolution fusion | flops 545783808 | bytes 6300928 | tf_op jit(solution)/shard_map/while/body/eval_jaxpr/while/body/eval_jaxpr/hkq,khd->qhd/dot_general | solution.py:47
  192.2 3.5 %bitcast_add_fusion.2 = f32[512,8,128]{0,2,1:T(8,128)S(1)} fusion(f32[512,8,128]{0,2,1:T(8,128)S(1)} %get-tuple-element.679, bf16[512,8,128]{2,0,1:T(8,128)(2,1)} %get-tuple-element.694, f32[8,256]{1,0:T(8,128)S(1)} %dynamic-slice_bitcast_fusion.2, pred[256]{0:T(512)(128)(4,1)S(1)} %dynamic_slice.64, bf16[1024,8,128]{2,0,1:T(8,128)(2,1)} %get-tuple-element.693, ...), kind=kOutput, calls=%fused_computation.3.clone.1 | convolution fusion | flops 545783808 | bytes 6300928 | tf_op jit(solution)/shard_map/while/body/eval_jaxpr/while/body/eval_jaxpr/hkq,khd->qhd/dot_general | solution.py:47
  195.8 3.5 %bitcast_add_fusion.2 = f32[512,8,128]{0,2,1:T(8,128)S(1)} fusion(f32[512,8,128]{0,2,1:T(8,128)S(1)} %get-tuple-element.679, bf16[512,8,128]{2,0,1:T(8,128)(2,1)} %get-tuple-element.694, f32[8,256]{1,0:T(8,128)S(1)} %dynamic-slice_bitcast_fusion.2, pred[256]{0:T(512)(128)(4,1)S(1)} %dynamic_slice.64, bf16[1024,8,128]{2,0,1:T(8,128)(2,1)} %get-tuple-element.693, ...), kind=kOutput, calls=%fused_computation.3.clone.1 | convolution fusion | flops 545783808 | bytes 6300928 | tf_op jit(solution)/shard_map/while/body/eval_jaxpr/while/body/eval_jaxpr/hkq,khd->qhd/dot_general | solution.py:47
  199.5 3.5 %bitcast_add_fusion.2 = f32[512,8,128]{0,2,1:T(8,128)S(1)} fusion(f32[512,8,128]{0,2,1:T(8,128)S(1)} %get-tuple-element.679, bf16[512,8,128]{2,0,1:T(8,128)(2,1)} %get-tuple-element.694, f32[8,256]{1,0:T(8,128)S(1)} %dynamic-slice_bitcast_fusion.2, pred[256]{0:T(512)(128)(4,1)S(1)} %dynamic_slice.64, bf16[1024,8,128]{2,0,1:T(8,128)(2,1)} %get-tuple-element.693, ...), kind=kOutput, calls=%fused_computation.3.clone.1 | convolution fusion | flops 545783808 | bytes 6300928 | tf_op jit(solution)/shard_map/while/body/eval_jaxpr/while/body/eval_jaxpr/hkq,khd->qhd/dot_general | solution.py:47
  213.9 14.6 %while.39 = (s32[]{:T(128)}, f32[512,8,128]{0,2,1:T(8,128)S(1)}, bf16[1024,8,128]{0,2,1:T(8,128)(2,1)}, pred[1024]{0:T(1024)(128)(4,1)S(1)}, bf16[1024,8,128]{2,...) while((s32[]{:T(128)}, f32[512,8,128]{0,2,1:T(8,128)S(1)}, ...), condition=%wide.region_4.4_spmd, body=%wide.region_3.3_spmd.sunk | while | flops 545783808 | bytes 6317987 | solution.py:156
  213.9 3.5 %bitcast_add_fusion.2 = f32[512,8,128]{0,2,1:T(8,128)S(1)} fusion(f32[512,8,128]{0,2,1:T(8,128)S(1)} %get-tuple-element.679, bf16[512,8,128]{2,0,1:T(8,128)(2,1)} %get-tuple-element.694, f32[8,256]{1,0:T(8,128)S(1)} %dynamic-slice_bitcast_fusion.2, pred[256]{0:T(512)(128)(4,1)S(1)} %dynamic_slice.64, bf16[1024,8,128]{2,0,1:T(8,128)(2,1)} %get-tuple-element.693, ...), kind=kOutput, calls=%fused_computation.3.clone.1 | convolution fusion | flops 545783808 | bytes 6300928 | tf_op jit(solution)/shard_map/while/body/eval_jaxpr/while/body/eval_jaxpr/hkq,khd->qhd/dot_general | solution.py:47
  217.6 3.5 %bitcast_add_fusion.2 = f32[512,8,128]{0,2,1:T(8,128)S(1)} fusion(f32[512,8,128]{0,2,1:T(8,128)S(1)} %get-tuple-element.679, bf16[512,8,128]{2,0,1:T(8,128)(2,1)} %get-tuple-element.694, f32[8,256]{1,0:T(8,128)S(1)} %dynamic-slice_bitcast_fusion.2, pred[256]{0:T(512)(128)(4,1)S(1)} %dynamic_slice.64, bf16[1024,8,128]{2,0,1:T(8,128)(2,1)} %get-tuple-element.693, ...), kind=kOutput, calls=%fused_computation.3.clone.1 | convolution fusion | flops 545783808 | bytes 6300928 | tf_op jit(solution)/shard_map/while/body/eval_jaxpr/while/body/eval_jaxpr/hkq,khd->qhd/dot_general | solution.py:47
  221.2 3.5 %bitcast_add_fusion.2 = f32[512,8,128]{0,2,1:T(8,128)S(1)} fusion(f32[512,8,128]{0,2,1:T(8,128)S(1)} %get-tuple-element.679, bf16[512,8,128]{2,0,1:T(8,128)(2,1)} %get-tuple-element.694, f32[8,256]{1,0:T(8,128)S(1)} %dynamic-slice_bitcast_fusion.2, pred[256]{0:T(512)(128)(4,1)S(1)} %dynamic_slice.64, bf16[1024,8,128]{2,0,1:T(8,128)(2,1)} %get-tuple-element.693, ...), kind=kOutput, calls=%fused_computation.3.clone.1 | convolution fusion | flops 545783808 | bytes 6300928 | tf_op jit(solution)/shard_map/while/body/eval_jaxpr/while/body/eval_jaxpr/hkq,khd->qhd/dot_general | solution.py:47
  224.9 3.5 %bitcast_add_fusion.2 = f32[512,8,128]{0,2,1:T(8,128)S(1)} fusion(f32[512,8,128]{0,2,1:T(8,128)S(1)} %get-tuple-element.679, bf16[512,8,128]{2,0,1:T(8,128)(2,1)} %get-tuple-element.694, f32[8,256]{1,0:T(8,128)S(1)} %dynamic-slice_bitcast_fusion.2, pred[256]{0:T(512)(128)(4,1)S(1)} %dynamic_slice.64, bf16[1024,8,128]{2,0,1:T(8,128)(2,1)} %get-tuple-element.693, ...), kind=kOutput, calls=%fused_computation.3.clone.1 | convolution fusion | flops 545783808 | bytes 6300928 | tf_op jit(solution)/shard_map/while/body/eval_jaxpr/while/body/eval_jaxpr/hkq,khd->qhd/dot_general | solution.py:47
  230.1 52.8 %all_to_all.31 = bf16[8,128,1024]{2,1,0:T(8,128)(2,1)S(1)} all-to-all(bf16[8,128,1024]{2,1,0:T(8,128)(2,1)} %bitcast.86), channel_id=1, replica_groups=mesh['users'=64,'ctx'=8] {'ctx'}, dimensions={0} | all-to-all | bytes 4194304 | tf_op jit(solution)/shard_map/all_to_all | solution.py:33
  284.9 22.9 %all_to_all.32 = bf16[64,2,1024]{2,1,0:T(2,128)(2,1)S(1)} all-to-all(bf16[64,2,1024]{2,1,0:T(2,128)(2,1)S(1)} %reshape.200), channel_id=1, replica_groups=mesh['users'=64,'ctx'=8] {'users'}, dimensions={0} | all-to-all | bytes 524288 | tf_op jit(solution)/shard_map/all_to_all | solution.py:178
  (101 shorter events, 37.4 us)
Async XLA Ops:
  6.5 134.2 %copy-start = (f32[32,8]{0,1:T(8,128)S(1)}, f32[32,8]{0,1:T(8,128)}, u32[]{:S(2)}) copy-start(f32[32,8]{0,1:T(8,128)} %param.26) | copy-start | bytes 3076
  6.5 110.2 %all-gather.2.cloned.1.call-start = ((), (), s32[]{:S(2)}) async-start(), calls=%async_computation.6 | async-start | bytes 8519680 | tf_op jit(solution)/shard_map/all_gather | solution.py:103
  9.6 15.0 %copy-start.10 = (s32[64,1]{0,1:T(1,128)S(1)}, s32[64,1]{0,1:T(1,128)}, u32[]{:S(2)}) copy-start(s32[64,1]{0,1:T(1,128)} %param.17) | copy-start | bytes 772
  9.6 69.6 %copy-start.4 = (bf16[64,1024]{1,0:T(8,128)(2,1)S(1)}, bf16[64,1024]{1,0:T(8,128)(2,1)}, u32[]{:S(2)}) copy-start(bf16[64,1024]{1,0:T(8,128)(2,1)} %param.16) | copy-start | bytes 393220
  9.6 69.6 %copy-start.5 = (f32[1024]{0:T(1024)S(1)}, f32[1024]{0:T(1024)}, u32[]{:S(2)}) copy-start(f32[1024]{0:T(1024)} %param.20) | copy-start | bytes 12292
  9.6 69.6 %all-to-all-start.1 = ((bf16[64,16,1024]{2,1,0:T(8,128)(2,1)}), bf16[64,16,1024]{2,1,0:T(8,128)(2,1)S(1)}, u32[]{:S(2)}, u32[]{:S(2)}) async-start(bf16[64,16,1024]{2,1,0:T(8,128)(2,1)} %broadcast_in_dim.96), calls=%async_computation.1 | async-start | bytes 4194304 | tf_op jit(solution)/shard_map/all_to_all | solution.py:12
  24.6 63.1 %copy-start.11 = (s32[64]{0:T(128)S(1)}, s32[64]{0:T(128)}, u32[]{:S(2)}) copy-start(s32[64]{0:T(128)} %param.18) | copy-start | bytes 772
  24.8 91.9 %copy-start.7 = (s32[64]{0:T(128)}, s32[64]{0:T(128)S(1)}, u32[]{:S(2)}) copy-start(s32[64]{0:T(128)S(1)} %multiply_add_fusion) | copy-start | bytes 772
  80.7 22.4 %all-to-all-start.2 = ((bf16[64,2,1024]{2,1,0:T(2,128)(2,1)}), bf16[64,2,1024]{2,1,0:T(2,128)(2,1)S(1)}, u32[]{:S(2)}, u32[]{:S(2)}) async-start(bf16[64,2,1024]{2,1,0:T(2,128)(2,1)} %reshape.196), calls=%async_computation.2 | async-start | bytes 524288 | tf_op jit(solution)/shard_map/all_to_all | solution.py:90
  103.1 19.4 %all-to-all-start = ((bf16[64,1,2]{2,1,0:T(2,128)(2,1)}), bf16[64,1,2]{2,1,0:T(2,128)(2,1)S(1)}, u32[]{:S(2)}, u32[]{:S(2)}) async-start(bf16[64,1,2]{2,1,0:T(2,128)(2,1)} %convert_element_type.88), calls=%async_computation | async-start | bytes 65536 | tf_op jit(solution)/shard_map/all_to_all | solution.py:97
  121.5 1.0 copy-start.1
  124.2 55.1 %all-to-all-start.3 = ((bf16[8,128,1024]{2,1,0:T(8,128)(2,1)}), bf16[8,128,1024]{2,1,0:T(8,128)(2,1)}, u32[]{:S(2)}, u32[]{:S(2)}) async-start(bf16[8,128,1024]{2,1,0:T(8,128)(2,1)} %stack.2), calls=%async_computation.3 | async-start | bytes 4194304 | tf_op jit(solution)/shard_map/all_to_all | solution.py:161
  136.8 3.9 %copy-start.9 = (s32[1,1024]{1,0:T(1,128)S(1)}, s32[1,1024]{1,0:T(1,128)}, u32[]{:S(2)}) copy-start(s32[1,1024]{1,0:T(1,128)} %param.25) | copy-start | bytes 12292
  179.3 3.4 %copy-start.2 = (bf16[128,8,128]{2,0,1:T(8,128)(2,1)}, bf16[128,8,128]{2,0,1:T(8,128)(2,1)S(1)}, u32[]{:S(2)}) copy-start(bf16[128,8,128]{2,0,1:T(8,128)(2,1)S(1)} %get-tuple-element.743) | copy-start | bytes 786436 | tf_op jit(solution)/shard_map/while
  203.6 1.1 copy-start.3
  204.7 3.4 %copy-start.2 = (bf16[128,8,128]{2,0,1:T(8,128)(2,1)}, bf16[128,8,128]{2,0,1:T(8,128)(2,1)S(1)}, u32[]{:S(2)}) copy-start(bf16[128,8,128]{2,0,1:T(8,128)(2,1)S(1)} %get-tuple-element.743) | copy-start | bytes 786436 | tf_op jit(solution)/shard_map/while
  229.0 1.1 copy-start.3
  283.0 0.7 copy-start.6
  283.5 24.5 %copy-start.8 = (s32[64]{0:T(128)S(1)}, s32[64]{0:T(128)}, u32[]{:S(2)}) copy-start(s32[64]{0:T(128)} %copy-done.7) | copy-start | bytes 772
Sparse Core Ops, SparseCore 0:
  10.7 105.9 all-gather.1
